TPU v7x, 32 devices: a whole 2x2x4 slice. The times are simulated.
32 devices in a mesh: grp: 4 (over x, core), dev: 8 (over z, y).
Axes of the slice: x: 2, y: 2, z: 4, core: 2. Of those that a mesh axis runs over, the one named last changes fastest.
Arguments:
- features: bfloat16 [4, 64, 32, 128], P('grp', None, 'dev'), may hold values from -6 to 6
- coarse_flow: bfloat16 [4, 4, 32, 128], P('grp', None, 'dev'), may hold values from -6 to 6
- target: bfloat16 [4, 2, 32, 128], P('grp', None, 'dev'), may hold values from -9 to 9
- valid_mask: int32 [4, 32, 128], P('grp', 'dev'), may hold values from 0 to 1, as said below
- weights: float32 [2306048], P('dev'), may hold values from -1 to 1, as said below
- momentum: float32 [2306048], P('dev'), may hold values from -39 to 39, as said below
- average: float32 [2306048], P('dev'), may hold values from -1 to 1, as said below
Outputs:
- flow: float32 [4, 2, 32, 128], P('grp', None, None, 'dev')
- feature_grad: float32 [4, 64, 32, 128], P('grp', None, 'dev')
- coarse_grad: float32 [4, 4, 32, 128], P('grp', None, 'dev')
- new_weights: float32 [2306048], P('dev')
- new_momentum: float32 [2306048], P('dev')
- new_average: float32 [2306048], P('dev')
- weights_bf16: bfloat16 [2306048], P('dev')
Inputs may be any that keep to these rules, and one draw needn't show every extreme that they name: `valid_mask`: 1 marks a pixel whose ground truth counts in the loss. `weights`: entries after 2304830 are zero. `momentum`: entries after 2304830 are zero. `average`: entries after 2304830 are zero.
All inputs are finite; a program needn't handle non-finite values.
Results may differ from a plain program's by a relative error of at most 0.013.
Values may be sent and summed in bfloat16 or wider, within the bound.
No kernel may reach another device: no remote copies, remote signals or barrier semaphores. Data moves between devices by JAX's collectives and lax.ppermute only.
A program may use at most 320 MiB of HBM per device.

v0:
```python
import jax
import jax.numpy as jnp
from jax import lax
from jax.sharding import PartitionSpec as P

FC = 32
SR = 4
NCOST = 81
D1 = 128
D2 = 128
D3 = 96
D4 = 64
D5 = 32
X1 = 128
X2 = 128
X3 = 128
X4 = 96
X5 = 64
X6 = 32
MARGIN = 8


SLOPE = 0.1
EPE_EPS = 0.01
MOMENTUM_RATE = 0.5
AVERAGE_DECAY = 0.5
LEARN_RATE = 0.001
DECAY_RATE = 0.0001
DILATIONS = (1, 2, 4, 8, 16, 1, 1)


def with_halo(cells, sides, width):
    for axis, dim in sides:
        count = lax.axis_size(axis)
        ends = count - 1
        head = lax.slice_in_dim(cells, 0, width, axis=dim)
        tail = lax.slice_in_dim(cells, cells.shape[dim] - width, cells.shape[dim], axis=dim)
        cells = jnp.concatenate(
            [
                lax.ppermute(tail, axis, [(i, (i + 1) % count) for i in range(ends)]),
                cells,
                lax.ppermute(head, axis, [((i + 1) % count, i) for i in range(ends)]),
            ],
            axis=dim,
        )
    return cells


def shortened(shard):
    return jax.tree.map(lambda a: a.astype(jnp.bfloat16) if a.dtype == jnp.float32 else a, shard)


def layer_table():
    layers = []
    channels = (2 * SR + 1) ** 2 + FC + 4
    for outgoing in (D1, D2, D3, D4, D5):
        layers.append((channels, outgoing, 1))
        channels = channels + outgoing
    layers.append((channels, 2, 1))
    for outgoing, dilation in zip((X1, X2, X3, X4, X5, X6, 2), DILATIONS):
        layers.append((channels, outgoing, dilation))
        channels = outgoing
    return layers


def unpack(flat_values):
    pieces = []
    offset = 0
    for incoming, outgoing, dilation in layer_table():
        kernel_count = incoming * outgoing * 9
        kernel = flat_values[offset : offset + kernel_count].reshape(outgoing, incoming, 3, 3)
        offset = offset + kernel_count
        biases = flat_values[offset : offset + outgoing]
        offset = offset + outgoing
        pieces.append((kernel, biases, dilation))
    return pieces


def leaky(values):
    return SLOPE * values + (1.0 - SLOPE) * jax.nn.silu(values)


def leaky_slope(values):
    logistic = jax.nn.sigmoid(values)
    return SLOPE + (1.0 - SLOPE) * (logistic + values * logistic * (1.0 - logistic))


def conv_forward(activations, kernel, biases, dilation):
    result = lax.conv_general_dilated(
        activations,
        kernel,
        (1, 1),
        ((dilation, dilation), (dilation, dilation)),
        rhs_dilation=(dilation, dilation),
        dimension_numbers=("NCHW", "OIHW", "NCHW"),
        preferred_element_type=jnp.float32,
    )
    return result + biases.astype(jnp.float32)[None, :, None, None]


def conv_input_grad(through, kernel, dilation):
    return lax.conv_general_dilated(
        through,
        jnp.flip(kernel, (2, 3)),
        (1, 1),
        ((dilation, dilation), (dilation, dilation)),
        rhs_dilation=(dilation, dilation),
        dimension_numbers=("NCHW", "IOHW", "NCHW"),
        preferred_element_type=jnp.float32,
    )


def conv_kernel_grad(activations, through, dilation):
    return lax.conv_general_dilated(
        activations,
        through,
        (dilation, dilation),
        ((dilation, dilation), (dilation, dilation)),
        dimension_numbers=("CNHW", "IOHW", "CNHW"),
        preferred_element_type=jnp.float32,
    )


def bias_grad(through):
    return jnp.sum(through, axis=(0, 2, 3), dtype=jnp.float32)


def correlate(first_map, second_map):
    padded = jnp.pad(second_map, ((0, 0), (0, 0), (SR, SR), (SR, SR)))
    height = first_map.shape[2]
    breadth = first_map.shape[3]
    volume = []
    for row_shift in range(2 * SR + 1):
        for col_shift in range(2 * SR + 1):
            window = padded[:, :, row_shift : row_shift + height, col_shift : col_shift + breadth]
            volume.append(jnp.mean(first_map * window, axis=1))
    return jnp.stack(volume, axis=1)


def correlate_grad(first_map, second_map, volume_grad):
    padded = jnp.pad(second_map, ((0, 0), (0, 0), (SR, SR), (SR, SR)))
    height = first_map.shape[2]
    breadth = first_map.shape[3]
    extent = 2 * SR + 1
    first_grad = jnp.zeros_like(first_map)
    second_grad = jnp.zeros_like(padded)
    for row_shift in range(extent):
        for col_shift in range(extent):
            weight_map = volume_grad[:, row_shift * extent + col_shift][:, None] / FC
            window = padded[:, :, row_shift : row_shift + height, col_shift : col_shift + breadth]
            first_grad = first_grad + weight_map * window
            second_grad = second_grad.at[
                :, :, row_shift : row_shift + height, col_shift : col_shift + breadth
            ].add(weight_map * first_map)
    return (first_grad, second_grad[:, :, SR : SR + height, SR : SR + breadth])


def forward(patches, layers):
    first_map = patches[:, :FC].astype(jnp.float32)
    second_map = patches[:, FC : 2 * FC].astype(jnp.float32)
    raw_cost = correlate(first_map, second_map)
    stacked = jnp.concatenate(
        [leaky(raw_cost).astype(jnp.bfloat16), patches[:, :FC], patches[:, 2 * FC :]], axis=1
    )
    inputs_kept = []
    pre_kept = []
    for kernel, biases, dilation in layers[:5]:
        inputs_kept.append(stacked)
        preact = conv_forward(stacked, kernel, biases, dilation)
        pre_kept.append(preact)
        stacked = jnp.concatenate([leaky(preact).astype(jnp.bfloat16), stacked], axis=1)
    kernel, biases, dilation = layers[5]
    estimate = conv_forward(stacked, kernel, biases, dilation)
    current = stacked
    for kernel, biases, dilation in layers[6:12]:
        inputs_kept.append(current)
        preact = conv_forward(current, kernel, biases, dilation)
        pre_kept.append(preact)
        current = leaky(preact).astype(jnp.bfloat16)
    kernel, biases, dilation = layers[12]
    motion = estimate + conv_forward(current, kernel, biases, dilation)
    return (motion, (first_map, second_map, raw_cost, inputs_kept, pre_kept, stacked, current))


def backward(layers, stored, motion_grad):
    first_map, second_map, raw_cost, inputs_kept, pre_kept, stacked, current = stored
    rounded = motion_grad.astype(jnp.bfloat16)
    grads_out = [None] * 13
    kernel, biases, dilation = layers[12]
    grads_out[12] = (conv_kernel_grad(current, rounded, dilation), bias_grad(rounded))
    running = conv_input_grad(rounded, kernel, dilation)
    for layer_at in range(11, 5, -1):
        kernel, biases, dilation = layers[layer_at]
        through = (running * leaky_slope(pre_kept[layer_at - 1])).astype(jnp.bfloat16)
        grads_out[layer_at] = (
            conv_kernel_grad(inputs_kept[layer_at - 1], through, dilation),
            bias_grad(through),
        )
        running = conv_input_grad(through, kernel, dilation)
    kernel, biases, dilation = layers[5]
    grads_out[5] = (conv_kernel_grad(stacked, rounded, dilation), bias_grad(rounded))
    running = running + conv_input_grad(rounded, kernel, dilation)
    for layer_at in range(4, -1, -1):
        kernel, biases, dilation = layers[layer_at]
        outgoing = kernel.shape[0]
        through = (running[:, :outgoing] * leaky_slope(pre_kept[layer_at])).astype(jnp.bfloat16)
        grads_out[layer_at] = (
            conv_kernel_grad(inputs_kept[layer_at], through, dilation),
            bias_grad(through),
        )
        running = running[:, outgoing:] + conv_input_grad(through, kernel, dilation)
    volume_grad = running[:, :NCOST] * leaky_slope(raw_cost)
    first_grad, second_grad = correlate_grad(first_map, second_map, volume_grad)
    patch_grad = jnp.concatenate(
        [first_grad + running[:, NCOST : NCOST + FC], second_grad, running[:, NCOST + FC :]], axis=1
    )
    flat_grad = jnp.concatenate(
        [
            jnp.concatenate([kernel_part.reshape(-1), bias_part])
            for kernel_part, bias_part in grads_out
        ]
    )
    return (patch_grad, flat_grad)


def update(weights, momentum, average, gradient):
    gradient = gradient + DECAY_RATE * weights
    renewed = MOMENTUM_RATE * momentum + gradient
    stepped = weights - LEARN_RATE * (gradient + MOMENTUM_RATE * renewed)
    return (stepped, renewed, AVERAGE_DECAY * average + (1.0 - AVERAGE_DECAY) * stepped)


def shards(features, coarse_flow, target, valid_mask, weights, momentum, average):
    gathered = lax.all_gather(weights.astype(jnp.bfloat16), "dev", axis=0, tiled=True)
    layers = unpack(gathered)
    counted = lax.psum(jnp.sum(valid_mask.astype(jnp.float32)), ("grp", "dev"))
    groups = lax.axis_size("grp")
    devices = lax.axis_size("dev")
    pixels = groups * features.shape[2] * devices * features.shape[3]
    weighting = pixels / counted
    joined = jnp.concatenate([features, coarse_flow], axis=1)
    marked = valid_mask.astype(jnp.bfloat16)[:, None]
    strip_data, strip_target, strip_mask = (
        lax.all_to_all(joined, "dev", split_axis=3, concat_axis=2, tiled=True),
        lax.all_to_all(target, "dev", split_axis=3, concat_axis=2, tiled=True),
        lax.all_to_all(marked, "dev", split_axis=3, concat_axis=2, tiled=True),
    )
    widened = with_halo(strip_data, (("dev", 3),), MARGIN)
    patches = jnp.pad(widened, ((0, 0), (0, 0), (MARGIN, MARGIN), (0, 0)))
    motion, stored = forward(patches, layers)
    height = strip_data.shape[2]
    breadth = strip_data.shape[3]
    interior = motion[:, :, MARGIN : MARGIN + height, MARGIN : MARGIN + breadth]
    mismatch = interior - strip_target.astype(jnp.float32)
    length = jnp.sqrt(jnp.sum(mismatch * mismatch, axis=1, keepdims=True) + EPE_EPS)
    motion_grad = weighting * strip_mask.astype(jnp.float32) * mismatch / length
    motion_grad = jnp.pad(motion_grad, ((0, 0), (0, 0), (MARGIN, MARGIN), (MARGIN, MARGIN)))
    patch_grad, flat_grad = backward(layers, stored, motion_grad)
    strip_grad = patch_grad[:, :, MARGIN : MARGIN + height]
    rim_grads = jnp.concatenate(
        [strip_grad[:, :, :, :MARGIN], strip_grad[:, :, :, MARGIN + breadth :]], axis=3
    )
    returned = with_halo(shortened(rim_grads), (("dev", 3),), MARGIN).astype(rim_grads.dtype)
    centre = strip_grad[:, :, :, MARGIN : MARGIN + breadth]
    centre = centre.at[:, :, :, :MARGIN].add(returned[:, :, :, :MARGIN])
    centre = centre.at[:, :, :, breadth - MARGIN :].add(returned[:, :, :, 3 * MARGIN :])
    row_grad = lax.all_to_all(
        shortened(centre), "dev", split_axis=2, concat_axis=3, tiled=True
    ).astype(centre.dtype)
    feature_grad = row_grad[:, : 2 * FC]
    coarse_grad = row_grad[:, 2 * FC :]
    padded_grad = jnp.pad(flat_grad, (0, gathered.shape[0] - flat_grad.shape[0]))
    shard_grad = lax.psum_scatter(
        padded_grad.astype(jnp.bfloat16), "dev", scatter_dimension=0, tiled=True
    )
    total_grad = lax.psum(shard_grad, "grp").astype(jnp.float32)
    new_weights, new_momentum, new_average = update(weights, momentum, average, total_grad)
    return (
        interior,
        feature_grad,
        coarse_grad,
        new_weights,
        new_momentum,
        new_average,
        new_weights.astype(jnp.bfloat16),
    )


def solution(mesh):
    in_specs = (
        P("grp", None, "dev", None),
        P("grp", None, "dev", None),
        P("grp", None, "dev", None),
        P("grp", "dev", None),
        P("dev"),
        P("dev"),
        P("dev"),
    )
    out_specs = (
        P("grp", None, None, "dev"),
        P("grp", None, "dev", None),
        P("grp", None, "dev", None),
        P("dev"),
        P("dev"),
        P("dev"),
        P("dev"),
    )
    return jax.shard_map(shards, mesh=mesh, in_specs=in_specs, out_specs=out_specs, check_vma=False)
```

profile of v0, /device:TPU:0, one launch (start us, length us, event | category | flops | bytes accessed | tf_op | source)
XLA Modules:
  0.0 3036.9 jit_solution(15434842955885081021)
XLA Ops:
  37.6 42.5 %psum.14 = f32[]{:T(128)} all-reduce(f32[]{:T(128)} %convert_reduce_fusion), channel_id=1, replica_groups=mesh['grp'=4,'dev'=8] {'grp','dev'}, use_global_device_ids=true, to_apply=%region_82.83 | all-reduce | flops 1 | bytes 8 | tf_op jit(solution)/shard_map/psum | solution.py:236
  113.9 32.8 %multiply_reduce_fusion = (f32[48,32]{1,0:T(8,128)S(1)}, f32[48,32]{1,0:T(8,128)}, f32[48,32]{1,0:T(8,128)}, f32[48,32]{1,0:T(8,128)}, f32[48,32]{1,0:T(8,128)}, /*index=5*/f32[48,32]{1,0:T(8,128)}, f32[48,32]{1,0:T(8,128)}) fusion(f32[1,32,48,32]{1,0,3,2:T(1,128)S(1)} %get-tuple-element.1498, bf16[1,68,32,32]{1,0,3,2:T(2,128)(2,1)S(1)} %copy.14395), kind=kLoop, calls=%fused_computation.440 | loop fusion | flops 1070592 | bytes 378880 | tf_op jit(solution)/shard_map/reduce_sum | solution.py:136
  146.8 26.9 multiply_reduce_fusion.1
  173.6 27.8 multiply_reduce_fusion.2
  201.4 28.2 multiply_reduce_fusion.3
  229.7 27.5 multiply_reduce_fusion.4
  257.2 27.2 multiply_reduce_fusion.5
  284.4 27.6 multiply_reduce_fusion.6
  312.0 28.3 multiply_reduce_fusion.7
  340.3 27.8 multiply_reduce_fusion.8
  368.1 27.9 multiply_reduce_fusion.9
  396.0 27.8 multiply_reduce_fusion.10
  423.8 27.8 multiply_reduce_fusion.11
  451.6 28.6 multiply_reduce_fusion.12
  576.8 83.8 %reduce.288 = bf16[8,288256]{1,0:T(8,128)(2,1)} reduce(bf16[8,1,288256]{2,1,0:T(2,128)(2,1)} %all-gather.3.cloned.1.call-done, bf16[]{:T(256)} %constant.2891), dimensions={1}, to_apply=%all-gather.reduce_sub_computation | reduce | bytes 9224194 | tf_op jit(solution)/shard_map/all_gather | solution.py:234
  799.9 73.8 %reshape.8460 = bf16[128,565,3,3]{3,2,1,0:T(4,128)(2,1)} reshape(bf16[650880]{0:T(1024)(128)(2,1)S(1)} %copy-done.34) | data formatting | bytes 2603520 | tf_op jit(solution)/shard_map/reshape | solution.py:71
  873.7 81.0 %copy.14515 = bf16[128,565,3,3]{0,1,3,2:T(8,128)(2,1)} copy(bf16[128,565,3,3]{3,2,1,0:T(4,128)(2,1)} %reshape.8460) | data formatting | bytes 2603520 | tf_op jit(solution)/shard_map/reshape | solution.py:71
  954.8 18.0 reshape.8458
  972.8 19.0 copy.14507
  991.8 31.1 %reshape.8457 = bf16[64,469,3,3]{3,2,1,0:T(4,128)(2,1)} reshape(bf16[270144]{0:T(1024)(128)(2,1)S(1)} %copy-done.55) | data formatting | bytes 1080576 | tf_op jit(solution)/shard_map/reshape | solution.py:71
  1022.8 29.9 copy.14501
  1052.7 37.0 %reshape.8456 = bf16[96,373,3,3]{3,2,1,0:T(4,128)(2,1)} reshape(bf16[322272]{0:T(1024)(128)(2,1)S(1)} %slice.4018) | data formatting | bytes 1289088 | tf_op jit(solution)/shard_map/reshape | solution.py:71
  1089.8 34.7 %copy.14495 = bf16[96,373,3,3]{1,0,3,2:T(8,128)(2,1)} copy(bf16[96,373,3,3]{3,2,1,0:T(4,128)(2,1)} %reshape.8456) | data formatting | bytes 1289088 | tf_op jit(solution)/shard_map/reshape | solution.py:71
  1124.4 32.5 %reshape.8455 = bf16[128,245,3,3]{3,2,1,0:T(4,128)(2,1)} reshape(bf16[282240]{0:T(1024)(128)(2,1)S(1)} %copy-done.53) | data formatting | bytes 1128960 | tf_op jit(solution)/shard_map/reshape | solution.py:71
  1156.9 36.2 %copy.14489 = bf16[128,245,3,3]{0,1,3,2:T(8,128)(2,1)} copy(bf16[128,245,3,3]{3,2,1,0:T(4,128)(2,1)} %reshape.8455) | data formatting | bytes 1128960 | tf_op jit(solution)/shard_map/reshape | solution.py:71
  1209.0 17.7 copy.14483
  1273.7 21.3 concatenate.362
  1309.9 25.8 concatenate.363
  1352.3 27.9 concatenate.364
  1437.1 51.5 %fusion.38 = f32[48,8,5,2]{1,3,2,0:T(2,128)S(1)} fusion(bf16[2,565,3,3]{1,0,3,2:T(2,128)(2,1)S(1)} %copy.14513, bf16[565,48,1,8,7]{0,1,4,3,2:T(8,128)(2,1)} %copy-done.41), kind=kOutput, calls=%fused_computation.51 | convolution fusion | flops 38510400 | bytes 3073140 | tf_op jit(solution)/shard_map/conv_general_dilated | solution.py:89
  1674.6 21.7 copy.14664
  1696.3 18.7 reshape.8483
  1721.6 43.9 %copy.14671 = bf16[128,245,3,3,1]{3,2,1,0,4:T(4,128)(2,1)} copy(bf16[128,245,3,3,1]{0,1,3,4,2:T(8,128)(2,1)S(1)} %fusion.126) | data formatting | bytes 1128960 | tf_op jit(solution)/shard_map/convert.45
  1765.5 36.4 %reshape.8484 = bf16[282240]{0:T(1024)(128)(2,1)} reshape(bf16[128,245,3,3,1]{3,2,1,0,4:T(4,128)(2,1)} %copy.14671) | data formatting | bytes 1128960 | tf_op jit(solution)/shard_map/reshape | solution.py:219
  1808.2 27.3 copy.14678
  1835.5 41.4 %reshape.8485 = bf16[322272]{0:T(1024)(128)(2,1)} reshape(bf16[96,373,3,3,1]{3,2,1,0,4:T(4,128)(2,1)} %copy.14678) | data formatting | bytes 1289088 | tf_op jit(solution)/shard_map/reshape | solution.py:219
  1885.4 24.3 copy.14685
  1909.8 34.9 %reshape.8486 = bf16[270144]{0:T(1024)(128)(2,1)} reshape(bf16[64,469,3,3,1]{3,2,1,0,4:T(4,128)(2,1)} %copy.14685) | data formatting | bytes 1080576 | tf_op jit(solution)/shard_map/reshape | solution.py:219
  1968.1 20.8 reshape.8487
  2025.1 99.8 %copy.14701 = bf16[128,565,3,3,1]{3,2,1,0,4:T(4,128)(2,1)} copy(bf16[128,565,3,3,1]{0,1,3,4,2:T(8,128)(2,1)S(1)} %fusion.73) | data formatting | bytes 2603520 | tf_op jit(solution)/shard_map/convert.40
  2124.9 81.7 %reshape.8489 = bf16[650880]{0:T(1024)(128)(2,1)} reshape(bf16[128,565,3,3,1]{3,2,1,0,4:T(4,128)(2,1)} %copy.14701) | data formatting | bytes 2603520 | tf_op jit(solution)/shard_map/reshape | solution.py:219
  2212.5 23.1 copy.14704
  2235.6 19.4 reshape.8490
  2255.0 23.1 copy.14706
  2278.1 19.3 reshape.8491
  2346.7 73.6 %concatenate.378 = bf16[2304830]{0:T(1024)(128)(2,1)} concatenate(bf16[134784]{0:T(1024)(128)(2,1)} %reshape.8483, bf16[128]{0:T(256)(128)(2,1)S(1)} %copy-done.366, bf16[282240]{0:T(1024)(128)(2,1)S(1)} %copy-done.54, bf16[128]{0:T(256)(128)(2,1)S(1)} %copy-done.367, bf16[322272]{0:T(1024)(128)(2,1)S(1)} %copy-done.52, bf16[96]{0:T(256)(128)(2,1)S(1)} %copy-done.364, ...), dimensions={0} | concatenate | bytes 9219320 | tf_op jit(solution)/shard_map/concatenate | solution.py:217
  2588.2 354.5 %bitcast_add_fusion = f32[1,32,48,32]{1,0,3,2:T(1,128)S(1)} fusion(f32[48,1,32,32]{3,1,2,0:T(1,128)S(1)} %copy-done.42, f32[48,32]{1,0:T(8,128)S(1)} %copy-done.198, f32[48,32]{1,0:T(8,128)S(1)} %copy-done.200, f32[48,32]{1,0:T(8,128)S(1)} %copy-done.201, f32[48,32]{1,0:T(8,128)S(1)} %copy-done.203, f32[48,32]{1,0:T(8,128)S(1)} %copy-done.205, ...), kind=kLoop, calls=%fused_computation.430 | loop fusion | flops 8011776 | bytes 1226752 | tf_op jit(solution)/shard_map/add | solution.py:215
  2997.2 28.5 all-reduce.9.cloned.1.call-done
  (1487 shorter events, 993.1 us)
Async XLA Ops:
  7.2 569.7 %all-gather.3.cloned.1.call-start = ((), (), s32[]{:S(2)}) async-start(), calls=%async_computation.5 | async-start | bytes 10377216 | tf_op jit(solution)/shard_map/all_gather | solution.py:234
  15.9 64.2 %copy-start.370 = (bf16[1,2,4,128]{3,2,1,0:T(4,128)(2,1)S(1)}, bf16[1,2,4,128]{3,2,1,0:T(4,128)(2,1)}, u32[]{:S(2)}) copy-start(bf16[1,2,4,128]{3,2,1,0:T(4,128)(2,1)} %param.175) | copy-start | bytes 6148
  16.7 14.3 all-to-all-start.1
  31.0 51.5 %all-to-all-start = ((bf16[1,68,4,128]{1,2,0,3:T(4,128)(2,1)}), bf16[1,68,4,128]{1,2,0,3:T(4,128)(2,1)S(1)}, u32[]{:S(2)}, u32[]{:S(2)}) async-start(bf16[1,68,4,128]{1,2,0,3:T(4,128)(2,1)} %pad_maximum_fusion.5), calls=%async_computation | async-start | bytes 262144 | tf_op jit(solution)/shard_map/all_to_all | solution.py:244
  82.5 13.8 all-to-all-start.2
  88.5 2901.0 %all-reduce.11.cloned.1.call-start = ((), (), s32[]{:S(2)}) async-start(), calls=%async_computation.6 | async-start | bytes 9224192
  88.7 8.5 collective-permute-start.1
  90.0 8.3 collective-permute-start
  98.9 470.8 %copy-start = (bf16[1,68,32,32]{1,0,3,2:T(2,128)(2,1)}, bf16[1,68,32,32]{1,0,3,2:T(2,128)(2,1)S(1)}, u32[]{:S(2)}) copy-start(bf16[1,68,32,32]{1,0,3,2:T(2,128)(2,1)S(1)} %copy.14395) | copy-start | bytes 417796
  101.1 350.5 %copy-start.3 = (f32[1,32,48,32]{1,0,3,2:T(1,128)}, f32[1,32,48,32]{1,0,3,2:T(1,128)S(1)}, u32[]{:S(2)}) copy-start(f32[1,32,48,32]{1,0,3,2:T(1,128)S(1)} %get-tuple-element.1498) | copy-start | bytes 589828
  101.1 469.8 %copy-start.7 = (bf16[1,32,48,32]{1,0,3,2:T(2,128)(2,1)}, bf16[1,32,48,32]{1,0,3,2:T(2,128)(2,1)S(1)}, u32[]{:S(2)}) copy-start(bf16[1,32,48,32]{1,0,3,2:T(2,128)(2,1)S(1)} %get-tuple-element.1499) | copy-start | bytes 294916
  1384.9 185.6 %copy-start.9 = (bf16[565,48,1,40]{0,1,3,2:T(8,128)(2,1)}, bf16[565,48,1,40]{0,1,3,2:T(8,128)(2,1)S(1)}, u32[]{:S(2)}) copy-start(bf16[565,48,1,40]{0,1,3,2:T(8,128)(2,1)S(1)} %get-tuple-element.1393) | copy-start | bytes 6508804
  1437.1 51.7 %copy-start.226 = (f32[48,8,5,2]{0,1,3,2:T(8,128)S(1)}, f32[48,8,5,2]{0,1,3,2:T(8,128)}, u32[]{:S(2)}) copy-start(f32[48,8,5,2]{0,1,3,2:T(8,128)} %copy.14531) | copy-start | bytes 46084
  1437.1 51.7 %copy-start.368 = (f32[2]{0:T(128)S(1)}, f32[2]{0:T(128)}, u32[]{:S(2)}) copy-start(f32[2]{0:T(128)} %get-tuple-element.1368) | copy-start | bytes 28
  1437.1 51.7 %copy-start.369 = (f32[2]{0:T(128)S(1)}, f32[2]{0:T(128)}, u32[]{:S(2)}) copy-start(f32[2]{0:T(128)} %get-tuple-element.1369) | copy-start | bytes 28
  1595.2 51.9 %copy-start.271 = (f32[48,32]{0,1:T(8,128)S(1)}, f32[48,32]{0,1:T(8,128)}, u32[]{:S(2)}) copy-start(f32[48,32]{0,1:T(8,128)} %get-tuple-element.1440) | copy-start | bytes 18436
  1598.1 51.8 %copy-start.267 = (f32[48,32]{0,1:T(8,128)S(1)}, f32[48,32]{0,1:T(8,128)}, u32[]{:S(2)}) copy-start(f32[48,32]{0,1:T(8,128)} %get-tuple-element.1436) | copy-start | bytes 18436
  1598.1 52.5 %copy-start.266 = (f32[48,32]{0,1:T(8,128)S(1)}, f32[48,32]{0,1:T(8,128)}, u32[]{:S(2)}) copy-start(f32[48,32]{0,1:T(8,128)} %get-tuple-element.1435) | copy-start | bytes 18436
  1598.1 53.2 %copy-start.265 = (f32[48,32]{0,1:T(8,128)S(1)}, f32[48,32]{0,1:T(8,128)}, u32[]{:S(2)}) copy-start(f32[48,32]{0,1:T(8,128)} %get-tuple-element.1434) | copy-start | bytes 18436
  1598.1 53.8 %copy-start.264 = (f32[48,32]{0,1:T(8,128)S(1)}, f32[48,32]{0,1:T(8,128)}, u32[]{:S(2)}) copy-start(f32[48,32]{0,1:T(8,128)} %get-tuple-element.1433) | copy-start | bytes 18436
  1598.1 54.5 %copy-start.263 = (f32[48,32]{0,1:T(8,128)S(1)}, f32[48,32]{0,1:T(8,128)}, u32[]{:S(2)}) copy-start(f32[48,32]{0,1:T(8,128)} %get-tuple-element.1432) | copy-start | bytes 18436
  1598.1 55.2 %copy-start.262 = (f32[48,32]{0,1:T(8,128)S(1)}, f32[48,32]{0,1:T(8,128)}, u32[]{:S(2)}) copy-start(f32[48,32]{0,1:T(8,128)} %get-tuple-element.1431) | copy-start | bytes 18436
  1598.1 55.9 %copy-start.261 = (f32[48,32]{0,1:T(8,128)S(1)}, f32[48,32]{0,1:T(8,128)}, u32[]{:S(2)}) copy-start(f32[48,32]{0,1:T(8,128)} %get-tuple-element.1430) | copy-start | bytes 18436
  1598.1 56.5 %copy-start.260 = (f32[48,32]{0,1:T(8,128)S(1)}, f32[48,32]{0,1:T(8,128)}, u32[]{:S(2)}) copy-start(f32[48,32]{0,1:T(8,128)} %get-tuple-element.1429) | copy-start | bytes 18436
  1598.1 57.2 %copy-start.259 = (f32[48,32]{0,1:T(8,128)S(1)}, f32[48,32]{0,1:T(8,128)}, u32[]{:S(2)}) copy-start(f32[48,32]{0,1:T(8,128)} %get-tuple-element.1428) | copy-start | bytes 18436
  1598.1 57.9 %copy-start.258 = (f32[48,32]{0,1:T(8,128)S(1)}, f32[48,32]{0,1:T(8,128)}, u32[]{:S(2)}) copy-start(f32[48,32]{0,1:T(8,128)} %get-tuple-element.1427) | copy-start | bytes 18436
  1598.1 58.6 %copy-start.257 = (f32[48,32]{0,1:T(8,128)S(1)}, f32[48,32]{0,1:T(8,128)}, u32[]{:S(2)}) copy-start(f32[48,32]{0,1:T(8,128)} %get-tuple-element.1426) | copy-start | bytes 18436
  1598.2 59.3 %copy-start.256 = (f32[48,32]{0,1:T(8,128)S(1)}, f32[48,32]{0,1:T(8,128)}, u32[]{:S(2)}) copy-start(f32[48,32]{0,1:T(8,128)} %get-tuple-element.1425) | copy-start | bytes 18436
  1598.2 59.9 %copy-start.255 = (f32[48,32]{0,1:T(8,128)S(1)}, f32[48,32]{0,1:T(8,128)}, u32[]{:S(2)}) copy-start(f32[48,32]{0,1:T(8,128)} %get-tuple-element.1424) | copy-start | bytes 18436
  1598.9 59.9 %copy-start.254 = (f32[48,32]{0,1:T(8,128)S(1)}, f32[48,32]{0,1:T(8,128)}, u32[]{:S(2)}) copy-start(f32[48,32]{0,1:T(8,128)} %get-tuple-element.1423) | copy-start | bytes 18436
  1599.6 59.9 %copy-start.253 = (f32[48,32]{0,1:T(8,128)S(1)}, f32[48,32]{0,1:T(8,128)}, u32[]{:S(2)}) copy-start(f32[48,32]{0,1:T(8,128)} %get-tuple-element.1422) | copy-start | bytes 18436
  1600.3 59.9 %copy-start.252 = (f32[48,32]{0,1:T(8,128)S(1)}, f32[48,32]{0,1:T(8,128)}, u32[]{:S(2)}) copy-start(f32[48,32]{0,1:T(8,128)} %get-tuple-element.1421) | copy-start | bytes 18436
  1601.0 59.9 %copy-start.251 = (f32[48,32]{0,1:T(8,128)S(1)}, f32[48,32]{0,1:T(8,128)}, u32[]{:S(2)}) copy-start(f32[48,32]{0,1:T(8,128)} %get-tuple-element.1420) | copy-start | bytes 18436
  1601.7 59.9 %copy-start.250 = (f32[48,32]{0,1:T(8,128)S(1)}, f32[48,32]{0,1:T(8,128)}, u32[]{:S(2)}) copy-start(f32[48,32]{0,1:T(8,128)} %get-tuple-element.1419) | copy-start | bytes 18436
  1602.4 59.9 %copy-start.249 = (f32[48,32]{0,1:T(8,128)S(1)}, f32[48,32]{0,1:T(8,128)}, u32[]{:S(2)}) copy-start(f32[48,32]{0,1:T(8,128)} %get-tuple-element.1418) | copy-start | bytes 18436
  1603.0 59.9 %copy-start.248 = (f32[48,32]{0,1:T(8,128)S(1)}, f32[48,32]{0,1:T(8,128)}, u32[]{:S(2)}) copy-start(f32[48,32]{0,1:T(8,128)} %get-tuple-element.1417) | copy-start | bytes 18436
  1603.7 59.9 %copy-start.247 = (f32[48,32]{0,1:T(8,128)S(1)}, f32[48,32]{0,1:T(8,128)}, u32[]{:S(2)}) copy-start(f32[48,32]{0,1:T(8,128)} %get-tuple-element.1416) | copy-start | bytes 18436
  1604.4 59.9 %copy-start.246 = (f32[48,32]{0,1:T(8,128)S(1)}, f32[48,32]{0,1:T(8,128)}, u32[]{:S(2)}) copy-start(f32[48,32]{0,1:T(8,128)} %get-tuple-element.1415) | copy-start | bytes 18436
  1605.1 59.9 %copy-start.245 = (f32[48,32]{0,1:T(8,128)S(1)}, f32[48,32]{0,1:T(8,128)}, u32[]{:S(2)}) copy-start(f32[48,32]{0,1:T(8,128)} %get-tuple-element.1414) | copy-start | bytes 18436
  1605.8 59.9 %copy-start.244 = (f32[48,32]{0,1:T(8,128)S(1)}, f32[48,32]{0,1:T(8,128)}, u32[]{:S(2)}) copy-start(f32[48,32]{0,1:T(8,128)} %get-tuple-element.1413) | copy-start | bytes 18436
  1606.5 59.9 %copy-start.243 = (f32[48,32]{0,1:T(8,128)S(1)}, f32[48,32]{0,1:T(8,128)}, u32[]{:S(2)}) copy-start(f32[48,32]{0,1:T(8,128)} %get-tuple-element.1412) | copy-start | bytes 18436
  1607.2 59.9 %copy-start.242 = (f32[48,32]{0,1:T(8,128)S(1)}, f32[48,32]{0,1:T(8,128)}, u32[]{:S(2)}) copy-start(f32[48,32]{0,1:T(8,128)} %get-tuple-element.1411) | copy-start | bytes 18436
  1614.2 56.3 %copy-start.39 = (f32[48,8,5,32]{3,1,2,0:T(8,128)S(1)}, f32[48,8,5,32]{3,1,2,0:T(8,128)}, u32[]{:S(2)}) copy-start(f32[48,8,5,32]{3,1,2,0:T(8,128)} %slice.4165) | copy-start | bytes 737284
  2124.9 81.7 %copy-start.71 = (bf16[48,8,5,128]{3,1,2,0:T(8,128)(2,1)S(1)}, bf16[48,8,5,128]{3,1,2,0:T(8,128)(2,1)}, u32[]{:S(2)}) copy-start(bf16[48,8,5,128]{3,1,2,0:T(8,128)(2,1)} %get-tuple-element.1367) | copy-start | bytes 1474564
  2966.7 10.1 collective-permute-start.3
  2968.1 8.7 collective-permute-start.2
  2978.6 17.0 all-to-all-start.3
  2988.2 37.5 %all-reduce.9.cloned.1.call-start = ((), (), s32[]{:S(2)}) async-start(), calls=%async_computation.4 | async-start | bytes 1155072 | tf_op jit(solution)/shard_map/psum | solution.py:276
  (345 other events, 2908.6 us)
Sparse Core Ops, SparseCore 0:
  16.0 145.4 all-gather.2
  2426.5 170.9 all-reduce.10
  2992.0 33.7 all-reduce.8
where the time goes:
time: 3070 us; the launch traced here: 3040 us
  local copies, waits for them, and re-layouts  1620 us (53%)
  other arithmetic  1070 us (35%)
  matrix products  210 us (7%)
  blocking collectives  42.5 us (1%)
  starting transfers between devices  41.3 us (1%)
  waiting for transfers between devices  34.3 us (1%)
    reshape x26, local copies, waits for them, and re-layouts, unpack(): flat_values[offset:offset + kernel_count].reshape(outgoing, incoming, 3, 3)  535 us
    reduce_sum x14, other arithmetic, correlate(): volume.append(jnp.mean(first_map * window, axis=1))  379 us
    add x1, other arithmetic, backward(): first_grad + running[:, NCOST:NCOST + FC]  355 us
    another operation x22, local copies, waits for them, and re-layouts  302 us
    reshape x13, local copies, waits for them, and re-layouts, backward(): kernel_part.reshape(-1)  300 us
    scatter-add x80, other arithmetic, correlate_grad(): second_grad = second_grad.at[:, :, row_shift:row_shift + height, col_shif...  180 us
    concatenate x34, local copies, waits for them, and re-layouts, forward(): jnp.concatenate([leaky(preact).astype(jnp.bfloat16), stacked], axis=1)  120 us
    conv_general_dilated x13, matrix products, conv_forward(): lax.conv_general_dilated(activations, kernel, (1, 1), ((dilation, dilatio...  114 us
  transfers between devices with their start and end apart: 11, of which 5 were waited for; matrix products, arithmetic and copies ran while one was open for 34% of the time, Pallas kernels for 0%

commit v1 on v0

v1 whole, which is shorter than its diff:
```python
import jax
import jax.numpy as jnp
from jax import lax
from jax.experimental import pallas as pl
from jax.experimental.pallas import tpu as pltpu
from jax.sharding import PartitionSpec as P

FC = 32
SR = 4
EXT = 2 * SR + 1
NCOST = EXT * EXT
NS0 = NCOST + FC + 4
DENSE = (128, 128, 96, 64, 32)
CONTEXT = (128, 128, 128, 96, 64, 32, 2)
DILATIONS = (1, 2, 4, 8, 16, 1, 1)
MARGIN = 8

SLOPE = 0.1
EPE_EPS = 0.01
MOMENTUM_RATE = 0.5
AVERAGE_DECAY = 0.5
LEARN_RATE = 0.001
DECAY_RATE = 0.0001

LANES = 128
PH = 48
PW = 32
PX = PH * PW
RIM = 16 * PW
STRIP = 128
MT = 512
PITCH = 40
F32 = jnp.float32
BF16 = jnp.bfloat16
NT = (((1,), (1,)), ((), ()))
TN = (((0,), (0,)), ((), ()))


def layer_table():
    places = [(NS0, 0, 0), (128, 1, 0), (128, 2, 0), (96, 3, 0), (64, 4, 0), (32, 3, 96)]
    layers = []
    offset = 0

    def add(pieces, outgoing, dilation, shift):
        nonlocal offset
        incoming = sum(n for n, _, _ in pieces)
        row = 9 * incoming
        segments = []
        at = 0
        for n, block, lane in pieces:
            segments.append((n, block, lane, offset + 9 * at))
            at += n
        layers.append(
            dict(
                out=outgoing,
                row=row,
                dil=dilation,
                shift=shift,
                segments=segments,
                blocks=1 + max(b for _, b, _ in pieces),
                bias=offset + row * outgoing,
                rows=LANES if outgoing == 2 else 9 * LANES,
            )
        )
        offset += row * outgoing + outgoing

    for i, outgoing in enumerate(DENSE):
        add(places[i::-1], outgoing, 1, 96 if i == 4 else 0)
    add(places[::-1], 2, 1, 0)
    add(places[::-1], CONTEXT[0], DILATIONS[0], 0)
    for i in range(1, 7):
        add([(CONTEXT[i - 1], 0, 0)], CONTEXT[i], DILATIONS[i], 0)
    return layers, offset


LAYERS, COUNT = layer_table()


def group_rows():
    at = 0
    groups = []
    for index, layer in enumerate(LAYERS):
        own = []
        for segment in layer["segments"]:
            own.append((at, segment))
            at += -(-layer["out"] // 16) * 16
        groups.append(own)
    return groups, -(-at // 64) * 64


GROUPS, GROUP_ROWS = group_rows()
TILES = 4


def iota(shape, dim):
    return lax.broadcasted_iota(jnp.int32, shape, dim)


def rows_at(start, size, step=8):
    return pl.ds(pl.multiple_of(start, step), size)


def sigmoid(v):
    return 0.5 * jnp.tanh(0.5 * v) + 0.5


def leaky(v):
    return SLOPE * v + (1.0 - SLOPE) * v * sigmoid(v)


def leaky_slope(v):
    s = sigmoid(v)
    return SLOPE + (1.0 - SLOPE) * (s + v * s * (1.0 - s))


def loop(count, body):
    def step(i, carry):
        body(i)
        return carry

    lax.fori_loop(0, count, step, 0)


def fill_order(order):
    for k in range(9):
        for m in range(9):
            row = iota((LANES, LANES), 0) + m * LANES
            col = iota((LANES, LANES), 1)
            order[m * LANES : (m + 1) * LANES, k * LANES : (k + 1) * LANES] = jnp.where(
                row == 9 * col + k, 1.0, 0.0
            ).astype(BF16)


def unpack_kernel(*refs):
    flat = refs[0]
    outs = refs[1:14]
    bias_out = refs[14]
    whole, slabs, aligned, result, order, heads = refs[15:]
    count = flat.shape[0]
    fill_order(order)

    def widen(i):
        whole[rows_at(i * 32, 32), :] = flat[rows_at(i * 32, 32, 32), :].astype(F32)

    loop(count // 32, widen)
    whole[count : count + 32, :] = jnp.zeros((32, LANES), F32)
    lane = iota((16, LANES), 1)

    def fetch(start, size):
        row = start >> 7
        off = start & 127
        turn = (128 - off) & 127
        here = pltpu.roll(whole[pl.ds(row, size), :], turn, 1)
        after = pltpu.roll(whole[pl.ds(row + 1, size), :], turn, 1)
        return jnp.where(lane[:size] < 128 - off, here, after)

    for index, layer in enumerate(LAYERS):
        outgoing = layer["out"]
        unroll = min(8, outgoing)
        for at, (n, block, place, start) in GROUPS[index]:
            first = start - 9 * place

            def take(i, first=first, unroll=unroll, row=layer["row"]):
                for u in range(unroll):
                    o = i * unroll + u
                    slabs[rows_at(o * 16, 16, 16), :] = fetch(first + o * row, 16)

            loop(outgoing // unroll, take)
            kept = -(-outgoing // 16) * 16
            for r in range(9):
                aligned[at : at + kept, r * LANES : (r + 1) * LANES] = slabs[
                    pl.ds(r, kept, stride=16), :
                ].astype(BF16)
        shift = layer["shift"]
        line = fetch(jnp.int32(layer["bias"] - shift), 8)[:1]
        spot = iota((1, LANES), 1)
        bias_out[index : index + 1, :] = jnp.where(
            (spot >= shift) & (spot < shift + outgoing), line, 0.0
        )
    bias_out[13:16, :] = jnp.zeros((3, LANES), F32)

    size = GROUP_ROWS // TILES

    def multiply(i):
        result[rows_at(i * size, size, 16), :] = jnp.dot(
            aligned[rows_at(i * size, size, 16), :], order[...], preferred_element_type=F32
        )

    loop(TILES, multiply)

    for index, layer in enumerate(LAYERS):
        outgoing = layer["out"]
        shift = layer["shift"]
        out = outs[index]
        if outgoing == 2:
            heads[...] = jnp.zeros_like(heads)
        elif outgoing < LANES:
            out[...] = jnp.zeros_like(out)
        for block in range(layer["blocks"]):
            for k in range(9):
                total = None
                for at, (n, own, place, _) in GROUPS[index]:
                    if own != block:
                        continue
                    tile = result[at : at + outgoing, k * LANES : (k + 1) * LANES]
                    spot = iota((outgoing, LANES), 1)
                    tile = jnp.where((spot >= place) & (spot < place + n), tile, 0.0)
                    total = tile if total is None else total + tile
                columns = slice(block * LANES, (block + 1) * LANES)
                if outgoing == 2:
                    heads[2 * k : 2 * k + 2, columns] = total
                else:
                    out[k * LANES + shift : k * LANES + shift + outgoing, columns] = total.astype(
                        BF16
                    )
        if outgoing == 2:
            out[...] = heads[:, : layer["blocks"] * LANES].astype(BF16)


def unpack(flat):
    count = flat.shape[0]
    shapes = [
        jax.ShapeDtypeStruct((layer["rows"], layer["blocks"] * LANES), BF16) for layer in LAYERS
    ] + [jax.ShapeDtypeStruct((16, LANES), F32)]
    return pl.pallas_call(
        unpack_kernel,
        out_shape=shapes,
        scratch_shapes=[
            pltpu.VMEM((count + 32, LANES), F32),
            pltpu.VMEM((16 * LANES, LANES), F32),
            pltpu.VMEM((GROUP_ROWS, 9 * LANES), BF16),
            pltpu.VMEM((GROUP_ROWS, 9 * LANES), F32),
            pltpu.VMEM((9 * LANES, 9 * LANES), BF16),
            pltpu.VMEM((LANES, 5 * LANES), F32),
        ],
        compiler_params=pltpu.CompilerParams(vmem_limit_bytes=58 * 2**20),
        name="unpack_weights",
    )(flat)


def pack_kernel(*refs):
    grads = refs[:13]
    bias_in = refs[13]
    flat = refs[14]
    whole, slabs, gathered, result, order, heads = refs[15:]
    count = flat.shape[0]
    fill_order(order)
    for index, layer in enumerate(LAYERS):
        outgoing = layer["out"]
        shift = layer["shift"]
        grad = grads[index]
        if outgoing == 2:
            heads[:LANES, : layer["blocks"] * LANES] = grad[...].astype(F32)
            heads[LANES:, :] = jnp.zeros((16, heads.shape[1]), F32)
        for at, (n, block, place, _) in GROUPS[index]:
            columns = slice(block * LANES, (block + 1) * LANES)
            for k in range(9):
                if outgoing == 2:
                    tile = heads[2 * k : 2 * k + 16, columns]
                    if place:
                        tile = pltpu.roll(tile, LANES - place, 1)
                    tile = tile.astype(BF16)
                else:
                    tile = grad[k * LANES + shift : k * LANES + shift + outgoing, columns]
                    if place:
                        tile = pltpu.roll(tile.astype(F32), LANES - place, 1).astype(BF16)
                gathered[at : at + tile.shape[0], k * LANES : (k + 1) * LANES] = tile

    size = GROUP_ROWS // TILES

    def multiply(i):
        result[rows_at(i * size, size, 16), :] = lax.dot_general(
            gathered[rows_at(i * size, size, 16), :], order[...], NT, preferred_element_type=F32
        )

    loop(TILES, multiply)

    lane = iota((8, LANES), 1)
    sub = iota((8, LANES), 0)

    def put(start, here, before, masked):
        row = start >> 7
        off = start & 127
        tile = jnp.where(lane >= off, pltpu.roll(here, off, 1), pltpu.roll(before, off, 1))
        if masked:
            pltpu.store(whole.at[pl.ds(row, 8), :], tile, mask=(sub > 0) | (lane >= off))
        else:
            whole[pl.ds(row + 8, 8), :] = tile

    for index, layer in enumerate(LAYERS):
        outgoing = layer["out"]
        region = outgoing * 16
        for s, (at, (n, _, _, _)) in enumerate(GROUPS[index]):
            for r in range(-(-9 * n // LANES)):
                slabs[pl.ds(s * region + 1 + r, outgoing, stride=16), :] = result[
                    at : at + outgoing, r * LANES : (r + 1) * LANES
                ]
        unroll = 2

        def place_rows(i, layer=layer, region=region, own=GROUPS[index], unroll=unroll):
            for u in range(unroll):
                o = i * unroll + u
                for s, (_, (n, _, _, start)) in enumerate(own):
                    base = s * region + o * 16
                    begin = start + o * layer["row"]
                    put(begin, slabs[pl.ds(base + 1, 8), :], slabs[pl.ds(base, 8), :], True)
                    if 9 * n > 7 * LANES:
                        put(begin, slabs[pl.ds(base + 9, 8), :], slabs[pl.ds(base + 8, 8), :], False)

        loop(outgoing // unroll, place_rows)
        line = bias_in[index : index + 1, :]
        if layer["shift"]:
            line = pltpu.roll(line, LANES - layer["shift"], 1)
        here = jnp.where(sub == 0, line, 0.0)
        before = jnp.where(sub == 1, line, 0.0)
        put(jnp.int32(layer["bias"]), here, before, True)
    end, off = COUNT // LANES, COUNT % LANES
    pltpu.store(
        whole.at[pl.ds(end, 8), :], jnp.zeros((8, LANES), F32), mask=(sub > 0) | (lane >= off)
    )
    left = count - end
    if left > 8:
        whole[end + 8 : count, :] = jnp.zeros((left - 8, LANES), F32)

    def narrow(i):
        flat[rows_at(i * 32, 32, 32), :] = whole[rows_at(i * 32, 32), :].astype(BF16)

    loop(count // 32, narrow)


def pack(grads, bias, count):
    return pl.pallas_call(
        pack_kernel,
        out_shape=jax.ShapeDtypeStruct((count, LANES), BF16),
        scratch_shapes=[
            pltpu.VMEM((count + 32, LANES), F32),
            pltpu.VMEM((6 * 16 * LANES + 16, LANES), F32),
            pltpu.VMEM((GROUP_ROWS, 9 * LANES), BF16),
            pltpu.VMEM((GROUP_ROWS, 9 * LANES), F32),
            pltpu.VMEM((9 * LANES, 9 * LANES), BF16),
            pltpu.VMEM((LANES + 16, 5 * LANES), F32),
        ],
        compiler_params=pltpu.CompilerParams(vmem_limit_bytes=62 * 2**20),
        name="pack_gradients",
    )(*grads, bias)


ROWS4 = 4 * PW
SEC_ROWS = (PH + 2 * SR) * PITCH + LANES


def load_second(joined, second):
    second[...] = jnp.zeros_like(second)
    keep = iota((PW, LANES), 1) < FC
    for y in range(MARGIN, PH - MARGIN):
        row = joined[y * PW : (y + 1) * PW, :].astype(F32)
        row = jnp.where(keep, pltpu.roll(row, LANES - FC, 1), 0.0)
        at = (y + SR) * PITCH + 8
        second[at : at + PW, :] = row


def band_shift(dy, third):
    return EXT * dy - PITCH * third - (8 - SR)


def correlate_kernel(received, stack0, cost, joined, second):
    joined[...] = jnp.zeros_like(joined)
    blocks = received.shape[0]
    for s in range(blocks):
        tile = received[s].astype(F32).T
        joined[RIM // 2 + s * ROWS4 : RIM // 2 + (s + 1) * ROWS4, :] = tile.astype(BF16)
    load_second(joined, second)
    row = iota((ROWS4, ROWS4), 0)
    col = iota((ROWS4, ROWS4), 1)
    flip = jnp.where((row // PW == col // PW) & (row % PW + col % PW == PW - 1), 1.0, 0.0).astype(
        BF16
    )
    lane = iota((ROWS4, LANES), 1)
    narrow = iota((PW, LANES), 1)

    def body(i):
        own = joined[rows_at(i * ROWS4, ROWS4, ROWS4), :]
        first = jnp.where(lane < FC, own.astype(F32), 0.0).astype(BF16)
        first = jnp.dot(flip, first, preferred_element_type=F32).astype(BF16)
        bands = []
        for g in range(4):
            window = second[rows_at((4 * i + 3 * g) * PITCH, LANES), :].astype(BF16)
            bands.append(lax.dot_general(first, window, NT, preferred_element_type=F32))
        pieces = []
        for yy in range(4):
            total = jnp.zeros((PW, LANES), F32)
            turned = [
                pltpu.roll(band[yy * PW : (yy + 1) * PW, :], 0, 1, stride=1, stride_axis=0)
                for band in bands
            ]
            for dy in range(EXT):
                t = yy + dy
                shift = (band_shift(dy, t % 3) - (PW - 1)) % LANES
                band = pltpu.roll(turned[t // 3], shift, 1)
                total = jnp.where((narrow >= EXT * dy) & (narrow < EXT * (dy + 1)), band, total)
            pieces.append(total * (1.0 / FC))
        total = jnp.concatenate(pieces, axis=0)
        high = total.astype(BF16)
        low = (total - high.astype(F32)).astype(BF16)
        total = jnp.dot(flip, high, preferred_element_type=F32) + jnp.dot(
            flip, low, preferred_element_type=F32
        )
        cost[rows_at(i * ROWS4, ROWS4, ROWS4), :] = total
        wide = own.astype(F32)
        filled = jnp.where(lane < NCOST, leaky(total), pltpu.roll(wide, NCOST, 1))
        coarse = pltpu.roll(wide, NCOST + FC - 2 * FC, 1)
        filled = jnp.where(lane >= NCOST + FC, coarse, filled)
        filled = jnp.where(lane < NS0, filled, 0.0)
        stack0[rows_at(i * ROWS4, ROWS4, ROWS4), :] = filled.astype(BF16)

    loop(PH // 4, body)


def correlate(received):
    return pl.pallas_call(
        correlate_kernel,
        out_shape=[
            jax.ShapeDtypeStruct((PX, LANES), BF16),
            jax.ShapeDtypeStruct((PX, LANES), F32),
            jax.ShapeDtypeStruct((PX, LANES), BF16),
        ],
        scratch_shapes=[pltpu.VMEM((SEC_ROWS, LANES), F32)],
        compiler_params=pltpu.CompilerParams(vmem_limit_bytes=32 * 2**20),
        name="correlate",
    )(received)


def correlate_back(joined, cost, dstack, second, dsecond, out):
    load_second(joined, second)
    dsecond[...] = jnp.zeros_like(dsecond)
    lane = iota((ROWS4, LANES), 1)
    narrow = iota((PW, LANES), 1)

    def body(i):
        rows = rows_at(i * ROWS4, ROWS4, ROWS4)
        own = joined[rows, :]
        first = jnp.where(lane < FC, own.astype(F32), 0.0).astype(BF16)
        grad = dstack[rows, :LANES]
        volume = grad * leaky_slope(cost[rows, :]) * (1.0 / FC)
        dfirst = jnp.zeros((ROWS4, LANES), F32)
        for g in range(4):
            pieces = []
            for yy in range(4):
                piece = jnp.zeros((PW, LANES), F32)
                own_rows = volume[yy * PW : (yy + 1) * PW, :]
                for t in range(3 * g, 3 * g + 3):
                    dy = t - yy
                    if dy < 0 or dy >= EXT:
                        continue
                    part = jnp.where(
                        (narrow >= EXT * dy) & (narrow < EXT * (dy + 1)), own_rows, 0.0
                    )
                    shift = (-band_shift(dy, t % 3)) % LANES
                    piece = piece + pltpu.roll(part, shift, 1)
                pieces.append(pltpu.roll(piece, 0, 1, stride=1, stride_axis=0))
            band = jnp.concatenate(pieces, axis=0).astype(BF16)
            at = rows_at((4 * i + 3 * g) * PITCH, LANES)
            dfirst = dfirst + jnp.dot(
                band, second[at, :].astype(BF16), preferred_element_type=F32
            )
            dsecond[at, :] += lax.dot_general(band, first, TN, preferred_element_type=F32)
        direct = pltpu.roll(grad, LANES - NCOST, 1)
        coarse = pltpu.roll(grad, LANES + 2 * FC - NCOST - FC, 1)
        filled = jnp.where(lane < FC, dfirst + direct, 0.0)
        filled = jnp.where((lane >= 2 * FC) & (lane < 2 * FC + 4), coarse, filled)
        dstack[rows, LANES : 2 * LANES] = filled

    loop(PH // 4, body)
    middle = iota((ROWS4, LANES), 1)
    for s in range((PH - 2 * MARGIN) // 4):
        pieces = []
        for yy in range(4):
            at = (MARGIN + 4 * s + yy + SR) * PITCH + 8
            pieces.append(dsecond[at : at + PW, :])
        other = pltpu.roll(jnp.concatenate(pieces, axis=0), FC, 1)
        start = (MARGIN + 4 * s) * PW
        tile = dstack[start : start + ROWS4, LANES : 2 * LANES]
        tile = jnp.where((middle >= FC) & (middle < 2 * FC), other, tile)
        out[s] = tile.T[: out.shape[1]].astype(BF16)


def network_kernel(*refs):
    stack0, cost, joined, weighting = refs[:4]
    kernels = refs[4:17]
    biases = refs[17]
    motion_out = refs[18]
    picture_out = refs[19]
    grads = refs[20:33]
    bias_out = refs[33]
    stack, ctx, pre, taps, moved, dstack, dcur, ghead, partial, second, dsecond = refs[34:]

    taps[:, :RIM, :] = jnp.zeros((9, RIM, LANES), F32)
    taps[:, RIM + PX :, :] = jnp.zeros((9, RIM, LANES), F32)
    moved[:, :RIM, :] = jnp.zeros((3, RIM, LANES), BF16)
    moved[:, RIM + PX :, :] = jnp.zeros((3, RIM, LANES), BF16)
    column = iota((STRIP, LANES), 0) % PW
    lane = iota((STRIP, LANES), 1)

    def strips(body):
        loop(PX // STRIP, lambda i: body(rows_at(i * STRIP, STRIP, STRIP), i * STRIP))

    def inside(tile, shift):
        if shift == 0:
            return tile
        valid = (column + shift >= 0) & (column + shift < PW)
        return jnp.where(valid, pltpu.roll(tile, (-shift) % STRIP, 0), 0.0)

    def multiply(load, kernel):
        def body(i):
            product = lax.dot_general(
                load(rows_at(i * MT, MT, MT)), kernel[...], NT, preferred_element_type=F32
            )
            for k in range(9):
                taps[k, rows_at(RIM + i * MT, MT, MT), :] = product[:, k * LANES : (k + 1) * LANES]

        loop(PX // MT, body)

    def collect(at, dilation):
        total = None
        for kx in range(3):
            part = None
            for ky in range(3):
                tile = taps[
                    ky * 3 + kx, rows_at(RIM + at + (ky - 1) * dilation * PW, STRIP, PW), :
                ]
                part = tile if part is None else part + tile
            part = inside(part, (kx - 1) * dilation)
            total = part if total is None else total + part
        return total

    stack[:, :LANES] = stack0[...]
    for index in range(5):
        layer = LAYERS[index]
        width = layer["blocks"] * LANES
        multiply(lambda rows, width=width: stack[rows, :width], kernels[index])

        def finish(rows, at, index=index, layer=layer):
            value = collect(at, 1) + biases[index : index + 1, :]
            pre[index, rows, :] = value
            fresh = leaky(value).astype(BF16)
            if index == 4:
                stack[rows, 3 * LANES : 4 * LANES] = stack[rows, 3 * LANES : 4 * LANES] + fresh
            else:
                stack[rows, (index + 1) * LANES : (index + 2) * LANES] = fresh

        strips(finish)
    for index in range(6, 12):
        layer = LAYERS[index]
        if index == 6:
            multiply(lambda rows: stack[rows, :], kernels[index])
        else:
            multiply(lambda rows, index=index: ctx[index - 7, rows, :], kernels[index])

        def finish(rows, at, index=index, layer=layer):
            value = collect(at, layer["dil"]) + biases[index : index + 1, :]
            pre[index - 1, rows, :] = value
            ctx[index - 6, rows, :] = leaky(value).astype(BF16)

        strips(finish)

    def head(i):
        rows = rows_at(i * MT, MT, MT)
        product = lax.dot_general(stack[rows, :], kernels[5][...], NT, preferred_element_type=F32)
        product = product + lax.dot_general(
            ctx[5, rows, :], kernels[12][...], NT, preferred_element_type=F32
        )
        taps[0, rows_at(RIM + i * MT, MT, MT), :] = product

    loop(PX // MT, head)

    row = iota((LANES, LANES), 0)
    col = iota((LANES, LANES), 1)
    used = (col < 18) & (row % 2 == col % 2)
    fold = jnp.where(used & (row < 18), 1.0, 0.0)
    spread = jnp.where(used & (row < 2), 1.0, 0.0).astype(BF16)
    pick = jnp.where(used & (row >= 2 * FC + 4) & (row < 2 * FC + 6), 1.0, 0.0).astype(BF16)
    marked = jnp.where(row == 2 * FC + 6, 1.0, 0.0).astype(BF16)
    both = (biases[5:6, :], biases[12:13, :])
    shared = sum(
        jnp.dot(jnp.broadcast_to(b, (8, LANES)).astype(BF16), spread, preferred_element_type=F32)
        for b in both
    )[:1]
    partial[...] = jnp.zeros_like(partial)

    def spread_grad(rows, at, grad, dilation):
        for kx in range(3):
            moved[kx, rows_at(RIM + at, STRIP, STRIP), :] = inside(
                grad, -(kx - 1) * dilation
            ).astype(BF16)

    def settle(rows, at):
        total = None
        for kx in range(3):
            part = None
            for ky in range(3):
                tile = taps[0, rows_at(RIM + at + (ky - 1) * PW, STRIP, PW), :]
                tile = jnp.where(lane // 2 == ky * 3 + kx, tile, 0.0)
                part = tile if part is None else part + tile
            part = inside(part, kx - 1)
            total = part if total is None else total + part
        motion = (
            jnp.dot(total, fold, preferred_element_type=F32, precision=lax.Precision.HIGHEST)
            + shared
        )
        motion_out[:, rows] = motion.T[: motion_out.shape[0]]
        own = joined[rows, :]
        aim = jnp.dot(own, pick, preferred_element_type=F32)
        mask = jnp.dot(own, marked, preferred_element_type=F32)
        mismatch = motion - aim
        square = mismatch * mismatch
        other = jnp.where(
            lane % 2 == 0, pltpu.roll(square, LANES - 1, 1), pltpu.roll(square, 1, 1)
        )
        length = jnp.sqrt(square + other + EPE_EPS)
        height = (iota((STRIP, LANES), 0) + at) // PW
        interior = (
            (height >= MARGIN)
            & (height < PH - MARGIN)
            & (column >= MARGIN)
            & (column < PW - MARGIN)
            & (lane < 18)
        )
        grad = jnp.where(interior, weighting[...] * mask * mismatch / length, 0.0)
        grad = grad.astype(BF16).astype(F32)
        partial[5] += grad.reshape(STRIP // 8, 8, LANES).sum(0)
        spread_grad(rows, at, grad, 1)

    strips(settle)
    partial[12] = partial[5]

    def choose(rows, at):
        total = None
        for kx in range(3):
            for ky in range(3):
                tile = moved[kx, rows_at(RIM + at - (ky - 1) * PW, STRIP, PW), :].astype(F32)
                tile = jnp.where(lane // 2 == ky * 3 + kx, tile, 0.0)
                total = tile if total is None else total + tile
        ghead[rows, :] = total.astype(BF16)

    strips(choose)
    grads[5][...] = lax.dot_general(
        ghead[...], stack[...], TN, preferred_element_type=F32
    ).astype(BF16)
    grads[12][...] = lax.dot_general(
        ghead[...], ctx[5], TN, preferred_element_type=F32
    ).astype(BF16)

    def head_back(i):
        rows = rows_at(i * MT, MT, MT)
        dstack[rows, :] = jnp.dot(ghead[rows, :], kernels[5][...], preferred_element_type=F32)
        dcur[rows, :] = jnp.dot(ghead[rows, :], kernels[12][...], preferred_element_type=F32)

    loop(PX // MT, head_back)

    def back(index, pre_at, load_grad, load_input, store):
        layer = LAYERS[index]
        dilation = layer["dil"]

        def through(rows, at):
            grad = load_grad(rows) * leaky_slope(pre[pre_at, rows, :])
            grad = grad.astype(BF16).astype(F32)
            partial[index] += grad.reshape(STRIP // 8, 8, LANES).sum(0)
            spread_grad(rows, at, grad, dilation)

        strips(through)

        def kernel_grad(ky):
            for kx in range(3):
                out_rows = rows_at((ky * 3 + kx) * LANES, LANES, LANES)
                tile = moved[kx, rows_at(RIM - (ky - 1) * dilation * PW, PX, PW), :]
                grads[index][out_rows, :] = lax.dot_general(
                    tile, load_input(), TN, preferred_element_type=F32
                ).astype(BF16)

        loop(3, kernel_grad)

        def input_grad(i):
            tiles = [
                moved[kx, rows_at(RIM + i * MT - (ky - 1) * dilation * PW, MT, PW), :]
                for ky in range(3)
                for kx in range(3)
            ]
            store(
                rows_at(i * MT, MT, MT),
                jnp.dot(
                    jnp.concatenate(tiles, axis=1), kernels[index][...], preferred_element_type=F32
                ),
            )

        loop(PX // MT, input_grad)

    def store_current(rows, value):
        dcur[rows, :] = value

    for index in range(11, 6, -1):
        back(
            index,
            index - 1,
            lambda rows: dcur[rows, :],
            lambda index=index: ctx[index - 7],
            store_current,
        )

    def store_stack(rows, value):
        dstack[rows, : value.shape[1]] += value

    back(6, 5, lambda rows: dcur[rows, :], lambda: stack[...], store_stack)
    for index in range(4, -1, -1):
        block = 3 if index == 4 else index + 1
        width = LAYERS[index]["blocks"] * LANES
        back(
            index,
            index,
            lambda rows, block=block: dstack[rows, block * LANES : (block + 1) * LANES],
            lambda width=width: stack[:, :width],
            store_stack,
        )
    bias_out[...] = partial[...].sum(1)
    correlate_back(joined, cost, dstack, second, dsecond, picture_out)


def network(stack0, cost, joined, weighting, kernels, biases, blocks, channels):
    grads = [jax.ShapeDtypeStruct(k.shape, BF16) for k in kernels]
    outs = pl.pallas_call(
        network_kernel,
        out_shape=[
            jax.ShapeDtypeStruct((8, PX), F32),
            jax.ShapeDtypeStruct((blocks, channels, LANES), BF16),
            *grads,
            jax.ShapeDtypeStruct((16, LANES), F32),
        ],
        scratch_shapes=[
            pltpu.VMEM((PX, 5 * LANES), BF16),
            pltpu.VMEM((6, PX, LANES), BF16),
            pltpu.VMEM((11, PX, LANES), F32),
            pltpu.VMEM((9, PX + 2 * RIM, LANES), F32),
            pltpu.VMEM((3, PX + 2 * RIM, LANES), BF16),
            pltpu.VMEM((PX, 5 * LANES), F32),
            pltpu.VMEM((PX, LANES), F32),
            pltpu.VMEM((PX, LANES), BF16),
            pltpu.VMEM((16, 8, LANES), F32),
            pltpu.VMEM((SEC_ROWS, LANES), F32),
            pltpu.VMEM((SEC_ROWS, LANES), F32),
        ],
        compiler_params=pltpu.CompilerParams(vmem_limit_bytes=62 * 2**20),
        name="network",
    )(stack0, cost, joined, weighting, *kernels, biases)
    return outs[0], outs[1], outs[2:15], outs[15]


def update(weights, momentum, average, gradient):
    gradient = gradient + DECAY_RATE * weights
    renewed = MOMENTUM_RATE * momentum + gradient
    stepped = weights - LEARN_RATE * (gradient + MOMENTUM_RATE * renewed)
    return (stepped, renewed, AVERAGE_DECAY * average + (1.0 - AVERAGE_DECAY) * stepped)


CHANNELS = 72


def shards(features, coarse_flow, target, valid_mask, weights, momentum, average):
    groups = lax.axis_size("grp")
    devices = lax.axis_size("dev")
    own_rows = features.shape[2]
    width = features.shape[3]
    breadth = width // devices
    height = own_rows * devices
    assert breadth + 2 * MARGIN == PW and height + 2 * MARGIN == PH
    gathered = lax.all_gather(weights.astype(BF16), "dev", axis=0, tiled=True)
    counted = lax.psum(jnp.sum(valid_mask.astype(F32)), ("grp", "dev"))
    weighting = groups * height * width / counted

    marked = valid_mask.astype(BF16)[:, None]
    spare = jnp.zeros((1, CHANNELS - 71, own_rows, width), BF16)
    picture = jnp.concatenate([features, coarse_flow, target, marked, spare], axis=1)[0]
    picture = jnp.pad(picture, ((0, 0), (0, 0), (MARGIN, MARGIN)))
    windows = jnp.stack([picture[:, :, t * breadth : t * breadth + PW] for t in range(devices)])
    received = lax.all_to_all(windows, "dev", split_axis=0, concat_axis=0, tiled=True)
    per = 4 // own_rows
    blocks = devices // per
    received = received.reshape(blocks, per, CHANNELS, own_rows * PW)
    received = jnp.swapaxes(received, 1, 2).reshape(blocks, CHANNELS, LANES)
    received = jnp.pad(received, ((0, 0), (0, LANES - CHANNELS), (0, 0)))

    stack0, cost, joined = correlate(received)
    unpacked = unpack(gathered.reshape(-1, LANES))
    kernels, biases = unpacked[:13], unpacked[13]
    motion, tiles, grads, bias_grads = network(
        stack0,
        cost,
        joined,
        jnp.full((1, LANES), weighting, F32),
        kernels,
        biases,
        blocks,
        CHANNELS,
    )
    flow = motion[:2].reshape(1, 2, PH, PW)[
        :, :, MARGIN : MARGIN + height, MARGIN : MARGIN + breadth
    ]
    flat_grad = pack(grads, bias_grads, gathered.shape[0] // LANES)

    tiles = tiles.reshape(blocks, CHANNELS, per, own_rows, PW)
    tiles = jnp.swapaxes(tiles, 1, 2).reshape(devices, CHANNELS, own_rows, PW)
    returned = lax.all_to_all(tiles, "dev", split_axis=0, concat_axis=0, tiled=True)
    returned = returned.astype(F32)
    wide = jnp.transpose(returned, (1, 2, 0, 3))
    centre = wide[..., MARGIN : MARGIN + breadth]
    left = wide[:, :, 1:, :MARGIN]
    right = wide[:, :, :-1, MARGIN + breadth :]
    none = ((0, 0), (0, 0))
    centre = centre + jnp.pad(left, (*none, (0, 1), (breadth - MARGIN, 0)))
    centre = centre + jnp.pad(right, (*none, (1, 0), (0, breadth - MARGIN)))
    row_grad = centre.reshape(1, CHANNELS, own_rows, width)
    feature_grad = row_grad[:, : 2 * FC]
    coarse_grad = row_grad[:, 2 * FC : 2 * FC + 4]

    shard_grad = lax.psum_scatter(
        flat_grad.reshape(-1), "dev", scatter_dimension=0, tiled=True
    )
    total_grad = lax.psum(shard_grad, "grp").astype(F32)
    new_weights, new_momentum, new_average = update(weights, momentum, average, total_grad)
    return (
        flow,
        feature_grad,
        coarse_grad,
        new_weights,
        new_momentum,
        new_average,
        new_weights.astype(BF16),
    )


def solution(mesh):
    in_specs = (
        P("grp", None, "dev", None),
        P("grp", None, "dev", None),
        P("grp", None, "dev", None),
        P("grp", "dev", None),
        P("dev"),
        P("dev"),
        P("dev"),
    )
    out_specs = (
        P("grp", None, None, "dev"),
        P("grp", None, "dev", None),
        P("grp", None, "dev", None),
        P("dev"),
        P("dev"),
        P("dev"),
        P("dev"),
    )
    return jax.shard_map(shards, mesh=mesh, in_specs=in_specs, out_specs=out_specs, check_vma=False)
```

time: 3070 us -> 704 us (0.23)
  local copies, waits for them, and re-layouts: 1620 us -> 35.9 us
  other arithmetic: 1070 us -> 90.1 us
  waiting for transfers between devices: 34.3 us -> 269 us
  Pallas kernels: 0 us -> 232 us
  matrix products: 210 us -> 0 us
    reshape x39 -> x2, local copies, waits for them, and re-layouts: 835 us -> 11.3 us  [the longest x1 11.2 us: shards(): unpacked = unpack(gathered.reshape(-1, LANES))]
    reduce_sum x24 -> x1, other arithmetic: 388 us -> 0.6 us  [shards(): counted = lax.psum(jnp.sum(valid_mask.astype(F32)), ('grp', 'dev'))]
    add x2 -> x1, other arithmetic: 355 us -> 0.03 us  [shards(): centre = centre + jnp.pad(right, (*none, (1, 0), (0, breadth - MARGIN)))]
    another operation x73 -> x2, local copies, waits for them, and re-layouts: 336 us -> 0.76 us  [the longest x1 0.62 us: shards(): jnp.stack([picture[:, :, t * breadth:t * breadth + PW] for t in range(dev...]
    pallas_call x0 -> x4, Pallas kernels: none -> 232 us  [the longest x1 104 us: network(): pl.pallas_call(network_kernel, out_shape=[jax.ShapeDtypeStruct((8, PX), F...]
    conv_general_dilated x39 -> x0, matrix products: 210 us -> none  [the longest x13 114 us: conv_forward(): lax.conv_general_dilated(activations, kernel, (1, 1), ((dilation, dilatio...]
    concatenate x43 -> x1, local copies, waits for them, and re-layouts: 197 us -> 0.27 us  [shards(): jnp.concatenate([features, coarse_flow, target, marked, spare], axis=1)[0]]
    scatter-add x82 -> x0, other arithmetic: 181 us -> none  [the longest x80 180 us: correlate_grad(): second_grad = second_grad.at[:, :, row_shift:row_shift + height, col_shif...]
  transfers between devices with their start and end apart: 11 -> 5, of which waited for: 5 -> 4; matrix products, arithmetic and copies ran while one was open for 34% -> 2% of each run, Pallas kernels for 0% -> 1%
where the time goes in v1:
time: 704 us; the launch traced here: 697 us
  waiting for transfers between devices  269 us (38%)
  Pallas kernels  232 us (33%)
  other arithmetic  90.1 us (13%)
  blocking collectives  43.3 us (6%)
  local copies, waits for them, and re-layouts  35.9 us (5%)
  between operations  15.8 us (2%)
  starting transfers between devices  10.8 us (2%)
    unnamed x4, waiting for transfers between devices  148 us
    pallas_call x1, Pallas kernels, network(): pl.pallas_call(network_kernel, out_shape=[jax.ShapeDtypeStruct((8, PX), F...  104 us
    all_gather x1, other arithmetic, shards(): gathered = lax.all_gather(weights.astype(BF16), 'dev', axis=0, tiled=True)  84.2 us
    all_gather x1, waiting for transfers between devices, shards(): gathered = lax.all_gather(weights.astype(BF16), 'dev', axis=0, tiled=True)  75.2 us
    pallas_call x1, Pallas kernels, pack(): pl.pallas_call(pack_kernel, out_shape=jax.ShapeDtypeStruct((count, LANES)...  67.4 us
    pallas_call x1, Pallas kernels, unpack(): pl.pallas_call(unpack_kernel, out_shape=shapes, scratch_shapes=[pltpu.VME...  52 us
    psum x1, blocking collectives, shards(): counted = lax.psum(jnp.sum(valid_mask.astype(F32)), ('grp', 'dev'))  43.3 us
    psum x1, waiting for transfers between devices, shards(): total_grad = lax.psum(shard_grad, 'grp').astype(F32)  31.3 us
  transfers between devices with their start and end apart: 5, of which 4 were waited for; matrix products, arithmetic and copies ran while one was open for 2% of the time, Pallas kernels for 1%

profile of v1, /device:TPU:0, one launch (start us, length us, event | category | flops | bytes accessed | tf_op | source)
XLA Modules:
  0.0 696.7 jit_solution(944126724625815228)
XLA Ops:
  7.2 1.3 convert_element_type.26
  8.6 7.3 %reshape.30 = bf16[1,1,288256]{2,1,0:T(2,128)(2,1)} reshape(bf16[288256]{0:T(1024)(128)(2,1)S(1)} %convert_element_type.26) | data formatting | bytes 1153024
  15.9 0.2 copy.35
  16.1 0.1 copy.32
  16.3 0.3 copy-done.10
  16.6 0.2 copy.33
  16.8 0.2 copy.34
  17.0 0.3 concatenate.3
  17.3 0.6 fusion.2
  17.9 0.6 fusion.10
  18.5 0.6 fusion.9
  19.1 0.6 fusion.8
  19.7 0.6 fusion.7
  20.4 0.6 fusion.6
  21.0 0.6 fusion.5
  21.6 0.6 fusion.4
  22.2 7.3 %all-to-all-start = ((bf16[8,72,4,32]{1,3,2,0:T(8,128)(2,1)}), bf16[8,72,4,32]{1,3,2,0:T(8,128)(2,1)S(1)}, u32[]{:S(2)}, u32[]{:S(2)}) async-start(bf16[8,72,4,32]{1,3,2,0:T(8,128)(2,1)} %fusion.4), calls=%async_computation | async-start | bytes 524288 | tf_op jit(solution)/shard_map/all_to_all | solution.py:783
  29.5 0.6 convert_reduce_fusion
  30.1 43.3 %psum.14 = f32[]{:T(128)} all-reduce(f32[]{:T(128)} %convert_reduce_fusion), channel_id=1, replica_groups=mesh['grp'=4,'dev'=8] {'grp','dev'}, use_global_device_ids=true, to_apply=%region_1.0 | all-reduce | flops 1 | bytes 8 | tf_op jit(solution)/shard_map/psum | solution.py:775
  74.2 0.1 copy.36
  74.4 8.9 %correlate.1 = (bf16[1536,128]{1,0:T(8,128)(2,1)S(1)}, f32[1536,128]{1,0:T(8,128)S(1)}, bf16[1536,128]{1,0:T(8,128)(2,1)S(1)}) custom-call(bf16[8,128,128]{2,1,0:T(8,128)(2,1)S(1)} %pad.17.received), custom_call_target="tpu_custom_call" | custom-call | tf_op jit(solution)/shard_map/correlate/pallas_call | solution.py:420
  83.2 0.9 copy-done
  84.1 0.7 copy-done.1
  84.9 0.7 copy-done.2
  85.6 75.2 %all-gather.3.cloned.1.call-done = bf16[8,1,288256]{2,1,0:T(2,128)(2,1)} async-done(((bf16[1,1,288256]{2,1,0:T(2,128)(2,1)}), bf16[8,1,288256]{2,1,0:T(2,128)(2,1)}) %all-gather.3.cloned.1.call-update) | async-done | bytes 4612112 | tf_op jit(solution)/shard_map/all_gather | solution.py:774
  160.8 84.2 %reduce = bf16[8,288256]{1,0:T(8,128)(2,1)} reduce(bf16[8,1,288256]{2,1,0:T(2,128)(2,1)} %all-gather.3.cloned.1.call-done, bf16[]{:T(256)} %constant.31), dimensions={1}, to_apply=%all-gather.reduce_sub_computation | reduce | bytes 9224194 | tf_op jit(solution)/shard_map/all_gather | solution.py:774
  245.0 11.2 %reshape.26.refs_0_ = bf16[18016,128]{1,0:T(8,128)(2,1)} reshape(bf16[8,288256]{1,0:T(8,128)(2,1)} %reduce) | data formatting | bytes 9224192 | tf_op jit(solution)/shard_map/reshape | solution.py:791
  256.3 52.0 %unpack_weights.1 = (bf16[1152,128]{1,0:T(8,128)(2,1)}, bf16[1152,256]{1,0:T(8,128)(2,1)}, bf16[1152,384]{1,0:T(8,128)(2,1)}, bf16[1152,512]{1,0:T(8,128)(2,1)},...) custom-call(bf16[18016,128]{1,0:T(8,128)(2,1)} %reshape.26.refs_0_), custom_call_target="tpu_custom_call" | custom-call | tf_op jit(solution)/shard_map/unpack_weights/pallas_call | solution.py:225
  308.3 0.5 broadcast_in_dim.11.refs_3_
  308.8 103.7 %network.1 = (f32[8,1536]{1,0:T(8,128)}, bf16[8,72,128]{2,1,0:T(8,128)(2,1)}, bf16[1152,128]{1,0:T(8,128)(2,1)}, bf16[1152,256]{1,0:T(8,128)(2,1)}, bf16[1152,38...) custom-call(bf16[1536,128]{1,0:T(8,128)(2,1)} %copy-done.1, ...), custom_call_target="tpu_custom_call" | custom-call | tf_op jit(solution)/shard_map/network/pallas_call | solution.py:729
  412.5 67.4 %pack_gradients.1 = bf16[18016,128]{1,0:T(8,128)(2,1)} custom-call(bf16[1152,128]{1,0:T(8,128)(2,1)} %get-tuple-element.59.refs_0_, bf16[1152,256]{1,0:T(8,128)(2,1)} %get-tuple-element.60.refs_1_, bf16[1152,384]{1,0:T(8,128)(2,1)} %get-tuple-element.61.refs_2_, bf16[1152,512]{1,0:T(8,128)(2,1)} %get-tuple-element.62.refs_3_, ...), custom_call_target="tpu_custom_call" | custom-call | tf_op jit(solution)/shard_map/pack_gradients/pallas_call | solution.py:332
  479.9 0.9 copy-done.7
  480.8 0.8 copy.37
  481.6 3.4 all-to-all-start.1
  485.1 0.6 dynamic-slice
  486.4 0.8 slice.59
  487.2 0.1 reshape.27
  487.3 0.7 copy.39
  488.0 14.1 %all-to-all-done.1 = bf16[8,72,4,32]{1,3,2,0:T(8,128)(2,1)S(1)} async-done(((bf16[8,72,4,32]{1,3,2,0:T(8,128)(2,1)}), bf16[8,72,4,32]{1,3,2,0:T(8,128)(2,1)S(1)}, u32[]{:S(2)}, u32[]{:S(2)}) %all-to-all-start.1) | async-done | bytes 147488 | tf_op jit(solution)/shard_map/all_to_all | solution.py:810
  502.2 148.2 %all-reduce.10.cloned.1.call-done = bf16[2306048]{0:T(1024)(128)(2,1)} async-done(((bf16[2306048]{0:T(1024)(128)(2,1)}), bf16[2306048]{0:T(1024)(128)(2,1)}) %all-reduce.10.cloned.1.call-update) | async-done | bytes 4612112
  650.4 2.2 dynamic-slice.1
  652.8 0.1 slice.77
  652.9 0.7 copy.41
  653.6 0.8 copy.40
  654.4 31.3 %all-reduce.8.cloned.1.call-done = bf16[288256]{0:T(1024)(128)(2,1)} async-done(((bf16[288256]{0:T(1024)(128)(2,1)}), bf16[288256]{0:T(1024)(128)(2,1)}) %all-reduce.8.cloned.1.call-update) | async-done | bytes 576528 | tf_op jit(solution)/shard_map/psum | solution.py:826
  685.7 2.6 fusion.11
  688.4 1.2 add_multiply_fusion
  689.6 0.2 copy-done.4
  (35 shorter events, 0.5 us)
Async XLA Ops:
  7.2 153.6 %all-gather.3.cloned.1.call-start = ((), (), s32[]{:S(2)}) async-start(), calls=%async_computation.3 | async-start | bytes 10377216 | tf_op jit(solution)/shard_map/all_gather | solution.py:774
  8.5 7.4 %copy-start.9 = (s32[1,4,128]{2,1,0:T(4,128)S(1)}, s32[1,4,128]{2,1,0:T(4,128)}, u32[]{:S(2)}) copy-start(s32[1,4,128]{2,1,0:T(4,128)} %param.10) | copy-start | bytes 6148
  8.5 7.6 %copy-start.8 = (bf16[1,64,4,128]{3,2,1,0:T(4,128)(2,1)S(1)}, bf16[1,64,4,128]{3,2,1,0:T(4,128)(2,1)}, u32[]{:S(2)}) copy-start(bf16[1,64,4,128]{3,2,1,0:T(4,128)(2,1)} %param.7) | copy-start | bytes 196612
  15.9 0.7 copy-start.10
  15.9 0.9 copy-start.11
  22.2 52.0 %all-to-all-start = ((bf16[8,72,4,32]{1,3,2,0:T(8,128)(2,1)}), bf16[8,72,4,32]{1,3,2,0:T(8,128)(2,1)S(1)}, u32[]{:S(2)}, u32[]{:S(2)}) async-start(bf16[8,72,4,32]{1,3,2,0:T(8,128)(2,1)} %fusion.4), calls=%async_computation | async-start | bytes 524288 | tf_op jit(solution)/shard_map/all_to_all | solution.py:783
  29.5 620.9 %all-reduce.10.cloned.1.call-start = ((), (), s32[]{:S(2)}) async-start(), calls=%async_computation.4 | async-start | bytes 9224192
  83.2 0.9 copy-start
  84.1 0.7 copy-start.1
  84.9 0.7 copy-start.2
  479.9 0.9 copy-start.7
  479.9 5.2 copy-start.12
  481.6 20.5 %all-to-all-start.1 = ((bf16[8,72,4,32]{1,3,2,0:T(8,128)(2,1)}), bf16[8,72,4,32]{1,3,2,0:T(8,128)(2,1)S(1)}, u32[]{:S(2)}, u32[]{:S(2)}) async-start(bf16[8,72,4,32]{1,3,2,0:T(8,128)(2,1)} %bitcast.11), calls=%async_computation.1 | async-start | bytes 524288 | tf_op jit(solution)/shard_map/all_to_all | solution.py:810
  485.1 200.7 %all-reduce.8.cloned.1.call-start = ((), (), s32[]{:S(2)}) async-start(), calls=%async_computation.2 | async-start | bytes 1155072 | tf_op jit(solution)/shard_map/psum | solution.py:826
  652.7 33.0 %copy-start.3 = (f32[288256]{0:T(1024)S(1)}, f32[288256]{0:T(1024)}, u32[]{:S(2)}) copy-start(f32[288256]{0:T(1024)} %param.11) | copy-start | bytes 3459076
  652.7 33.0 %copy-start.6 = (f32[288256]{0:T(1024)S(1)}, f32[288256]{0:T(1024)}, u32[]{:S(2)}) copy-start(f32[288256]{0:T(1024)} %param.12) | copy-start | bytes 3459076
  654.4 33.9 %copy-start.5 = (f32[288256]{0:T(1024)S(1)}, f32[288256]{0:T(1024)}, u32[]{:S(2)}) copy-start(f32[288256]{0:T(1024)} %param.13) | copy-start | bytes 3459076
  688.3 1.4 copy-start.4
Sparse Core Ops, SparseCore 0:
  16.0 144.7 all-gather.2
  480.0 170.3 all-reduce.9
  653.4 32.3 all-reduce.7
